TPU v7x, 256 devices: a whole 4x4x8 slice. The times are simulated.
256 devices in a mesh: doc: 16 (over z_lo, x), head: 8 (over z_hi, y), cuts: 2 (over core).
Axes of the slice: x: 4, y: 4, z: 8 (z_hi: 2, z_lo: 4; z = z_hi * 4 + z_lo), core: 2. Of those that a mesh axis runs over, the one named last changes fastest.
Arguments:
- inputs: bfloat16 [2, 16, 256, 4096], P('cuts', 'doc'), may hold values from -9 to 9
- weight_query: bfloat16 [4096, 2048], P(None, 'head'), may hold values from -1 to 1
- weight_key: bfloat16 [4096, 2048], P(None, 'head'), may hold values from -2 to 2
- weight_value: bfloat16 [4096, 2048], P(None, 'head'), may hold values from -0.09375 to 0.09375
- grad_output: bfloat16 [2, 16, 256, 2048], P('cuts', 'doc', None, 'head'), may hold values from -24 to 24
- partner_one: int32 [2, 16], P('cuts'), may hold values from 0 to 15, each once within a row
- partner_two: int32 [2, 16], P('cuts'), may hold values from 0 to 15, each once within a row
Outputs:
- grad_key: bfloat16 [2, 16, 256, 2048], P('cuts', 'doc', None, 'head')
- grad_value: bfloat16 [2, 16, 256, 2048], P('cuts', 'doc', None, 'head')
- grad_weight_query: float32 [4096, 2048], P(('doc', 'cuts'), 'head')
- grad_weight_key: float32 [4096, 2048], P(('doc', 'cuts'), 'head')
- grad_weight_value: float32 [4096, 2048], P(('doc', 'cuts'), 'head')
- grad_input: bfloat16 [2, 16, 4096, 256], P('cuts', 'doc', 'head')
Inputs may be any that keep to these rules, and one draw needn't show every extreme that they name: `partner_one`: each row is a permutation of the documents 0 to 15 of the slice. `partner_two`: each row is a permutation of the documents 0 to 15 of the slice.
All inputs are finite; a program needn't handle non-finite values.
Results may differ from a plain program's by a relative error of at most 0.033.
Values may be sent and summed in bfloat16 or wider, within the bound.
No kernel may reach another device: no remote copies, remote signals or barrier semaphores. Data moves between devices by JAX's collectives and lax.ppermute only.
A program may use at most 128 MiB of HBM per device.

v0:
```python
import math
import jax
import jax.numpy as jnp
from jax import lax
from jax.sharding import PartitionSpec as P

HD = 128


def per_device(
    inputs, weight_query, weight_key, weight_value, grad_output, partner_one, partner_two
):
    tokens = inputs[0, 0]
    length = tokens.shape[0]
    columns = weight_query.shape[1]
    head_count = columns // HD
    factor = 1.0 / math.sqrt(HD)
    doc_peers = lax.axis_size("doc")
    block_rows = length // doc_peers
    myself = lax.axis_index("doc")
    first_partner = partner_one[0]
    second_partner = partner_two[0]
    queries = jnp.dot(tokens, weight_query, preferred_element_type=jnp.float32).astype(jnp.bfloat16)
    key_rows = jnp.dot(tokens, weight_key, preferred_element_type=jnp.float32).astype(jnp.bfloat16)
    value_rows = jnp.dot(tokens, weight_value, preferred_element_type=jnp.float32).astype(
        jnp.bfloat16
    )
    key_value = jnp.concatenate([key_rows, value_rows], axis=1)
    chosen = jnp.stack([first_partner[myself], second_partner[myself]])
    offsets = jnp.arange(length, dtype=jnp.int32)
    start_kv = jnp.zeros((2, length, 2 * columns), jnp.bfloat16)
    segment = lax.all_gather(key_value, "doc", axis=0, tiled=True)
    amount = segment.shape[0]
    slot_rows = []
    for which_one in range(2):
        positions = chosen[which_one] * length + offsets
        inside = (positions >= 0) & (positions < amount)
        picked = jnp.take(segment, jnp.clip(positions, 0, amount - 1), axis=0)
        slot_rows.append(jnp.where(inside[:, None], picked, start_kv[which_one]))
    partner_kv = jnp.stack(slot_rows)
    keys_all = jnp.concatenate(
        [key_rows, partner_kv[0, :, :columns], partner_kv[1, :, :columns]], axis=0
    )
    keys_all = keys_all.reshape(3 * length, head_count, HD)
    values_all = jnp.concatenate(
        [value_rows, partner_kv[0, :, columns:], partner_kv[1, :, columns:]], axis=0
    )
    values_all = values_all.reshape(3 * length, head_count, HD)
    query_heads = queries.reshape(length, head_count, HD)
    dout_rows = grad_output[0, 0]
    dout_heads = dout_rows.reshape(length, head_count, HD)
    scores = (
        jnp.einsum("qhe,khe->hqk", query_heads, keys_all, preferred_element_type=jnp.float32)
        * factor
    )
    row_index = lax.broadcasted_iota(jnp.int32, (length, 3 * length), 0)
    col_index = lax.broadcasted_iota(jnp.int32, (length, 3 * length), 1)
    allowed = (col_index >= length) | (col_index <= row_index)
    scores = jnp.where(allowed[None], scores, -jnp.inf)
    maximum = jnp.max(scores, axis=-1, keepdims=True)
    exponent = jnp.exp(scores - maximum)
    totals = jnp.sum(exponent, axis=-1, keepdims=True)
    probability = exponent / totals
    rounded = probability.astype(jnp.bfloat16)
    attended = jnp.einsum("hqk,khe->qhe", rounded, values_all, preferred_element_type=jnp.float32)
    row_delta = jnp.sum(dout_heads.astype(jnp.float32) * attended, axis=-1)
    prob_grad = jnp.einsum(
        "qhe,khe->hqk", dout_heads, values_all, preferred_element_type=jnp.float32
    )
    score_grad = (probability * (prob_grad - row_delta.T[:, :, None])).astype(jnp.bfloat16)
    grad_query = (
        jnp.einsum("hqk,khe->qhe", score_grad, keys_all, preferred_element_type=jnp.float32)
        * factor
    )
    grad_query = grad_query.astype(jnp.bfloat16).reshape(length, columns)
    doc_numbers = jnp.arange(doc_peers, dtype=jnp.int32)
    grad_keys = (
        jnp.einsum("hqk,qhe->khe", score_grad, query_heads, preferred_element_type=jnp.float32)
        * factor
    )
    grad_values = jnp.einsum(
        "hqk,qhe->khe", rounded, dout_heads, preferred_element_type=jnp.float32
    )
    both_grads = jnp.concatenate(
        [grad_keys.reshape(3 * length, columns), grad_values.reshape(3 * length, columns)], axis=1
    )
    own_grad = both_grads[:length]
    outbound = both_grads[length:].reshape(2, doc_peers, block_rows, 2 * columns)
    received = lax.all_to_all(
        outbound.astype(jnp.bfloat16), "doc", split_axis=1, concat_axis=1, tiled=True
    ).astype(outbound.dtype)
    chosen_one = (first_partner[:, None] == doc_numbers[None, :]).astype(jnp.float32)
    chosen_two = (second_partner[:, None] == doc_numbers[None, :]).astype(jnp.float32)
    gathered = jnp.einsum("dt,dbf->tbf", chosen_one, received[0], precision=lax.Precision.HIGHEST)
    gathered = gathered + jnp.einsum(
        "dt,dbf->tbf", chosen_two, received[1], precision=lax.Precision.HIGHEST
    )
    returned = (
        lax.all_to_all(
            gathered.astype(jnp.bfloat16), "doc", split_axis=0, concat_axis=0, tiled=True
        )
        .astype(gathered.dtype)
        .reshape(length, 2 * columns)
    )
    kv_grad = own_grad + returned
    grad_key = kv_grad[:, :columns].astype(jnp.bfloat16)
    grad_value = kv_grad[:, columns:].astype(jnp.bfloat16)
    all_grads = jnp.concatenate([grad_query, grad_key, grad_value], axis=1)
    shared = lax.psum_scatter(
        lax.dot_general(
            tokens, all_grads, (((0,), (0,)), ((), ())), preferred_element_type=jnp.float32
        ).astype(jnp.bfloat16),
        ("doc", "cuts"),
        scatter_dimension=0,
        tiled=True,
    ).astype(jnp.float32)
    numbers = (((1,), (1,)), ((), ()))
    result = lax.dot_general(weight_query, grad_query, numbers, preferred_element_type=jnp.float32)
    result = result + lax.dot_general(
        weight_key, grad_key, numbers, preferred_element_type=jnp.float32
    )
    result = result + lax.dot_general(
        weight_value, grad_value, numbers, preferred_element_type=jnp.float32
    )
    input_rows = lax.psum_scatter(
        result.astype(jnp.bfloat16), "head", scatter_dimension=0, tiled=True
    ).astype(jnp.float32)
    return (
        grad_key.reshape(1, 1, length, columns),
        grad_value.reshape(1, 1, length, columns),
        shared[:, :columns],
        shared[:, columns : 2 * columns],
        shared[:, 2 * columns :],
        input_rows.astype(jnp.bfloat16).reshape(1, 1, input_rows.shape[0], length),
    )


def solution(mesh):
    in_specs = (
        P("cuts", "doc", None, None),
        P(None, "head"),
        P(None, "head"),
        P(None, "head"),
        P("cuts", "doc", None, "head"),
        P("cuts", None),
        P("cuts", None),
    )
    out_specs = (
        P("cuts", "doc", None, "head"),
        P("cuts", "doc", None, "head"),
        P(("doc", "cuts"), "head"),
        P(("doc", "cuts"), "head"),
        P(("doc", "cuts"), "head"),
        P("cuts", "doc", "head", None),
    )
    return jax.shard_map(
        per_device, mesh=mesh, in_specs=in_specs, out_specs=out_specs, check_vma=False
    )
```

profile of v0, /device:TPU:16, one launch (start us, length us, event | category | flops | bytes accessed | tf_op | source)
XLA Modules:
  0.0 437.8 jit_solution(7440671462932104760)
XLA Ops:
  7.2 1.5 copy-done
  8.8 2.7 fusion.20
  11.5 1.0 fusion.23
  12.5 0.7 pad_maximum_fusion.3
  13.6 0.6 fusion.61
  14.2 0.7 compare_and_fusion
  14.9 0.7 compare_and_fusion.2
  15.5 0.7 compare_and_fusion.1
  16.2 0.7 compare_and_fusion.3
  16.8 0.7 compare_select_fusion
  17.5 0.7 compare_select_fusion.1
  18.3 2.5 fusion.17
  20.8 84.0 %all-gather.2.cloned.1.call-done = bf16[4096,512]{0,1:T(8,128)(2,1)} async-done(((bf16[256,512]{0,1:T(8,128)(2,1)}), bf16[4096,512]{0,1:T(8,128)(2,1)}) %all-gather.2.cloned.1.call-update) | async-done | bytes 4194320 | tf_op jit(solution)/shard_map/all_gather | solution.py:32
  104.8 6.5 %copy.57 = bf16[4096,512]{1,0:T(8,128)(2,1)} copy(bf16[4096,512]{0,1:T(8,128)(2,1)} %all-gather.2.cloned.1.call-done) | data formatting | bytes 8388608 | tf_op jit(solution)/shard_map/all_gather | solution.py:32
  111.3 3.9 gather_fusion.1
  115.3 3.9 gather_fusion
  119.5 0.8 copy.69
  120.5 0.8 copy.68
  121.8 1.9 fusion.63
  123.7 1.6 fusion.29
  125.3 1.2 fusion.65
  126.5 1.4 copy.75
  127.9 1.6 fusion.26
  129.5 1.9 fusion.12
  131.4 0.9 copy-done.5
  132.3 1.2 convolution_multiply_fusion
  133.5 2.3 copy.74
  135.8 1.1 fusion.27
  137.0 19.8 %all_to_all.10 = bf16[2,16,16,512]{3,2,0,1:T(8,128)(2,1)S(1)} all-to-all(bf16[2,16,16,512]{3,2,0,1:T(8,128)(2,1)S(1)} %copy.76), channel_id=1, replica_groups=mesh['doc'=16,'head'=8,'cuts'=2] {'doc'}, dimensions={1} | all-to-all | bytes 1048576 | tf_op jit(solution)/shard_map/all_to_all | solution.py:89
  157.4 0.9 copy.79
  158.2 3.5 all-to-all-start.1
  162.0 1.6 fusion.16
  163.6 4.3 fusion.64
  167.9 3.8 all-to-all-done.1
  171.7 1.2 fusion.32
  172.9 0.5 copy-done.1
  173.4 3.1 convolution_add_fusion.1
  176.5 2.1 fusion.3
  178.7 4.5 %fusion.1 = bf16[4096,768]{0,1:T(8,128)(2,1)} fusion(bf16[1,1,256,4096]{3,2,1,0:T(8,128)(2,1)S(1)} %copy-done, bf16[256,512]{1,0:T(8,128)(2,1)S(1)} %fusion.32, bf16[256,256]{1,0:T(8,128)(2,1)S(1)} %copy.81), kind=kOutput, calls=%fused_computation.4 | convolution fusion | flops 1614544896 | bytes 8781824 | tf_op jit(solution)/shard_map/dot_general | solution.py:110
  183.2 8.6 %copy.91 = bf16[4096,768]{1,0:T(8,128)(2,1)} copy(bf16[4096,768]{0,1:T(8,128)(2,1)} %fusion.1) | data formatting | bytes 12582912
  191.9 0.7 slice_bitcast_fusion
  192.6 81.1 %reduce-scatter.5.cloned.1.call-done = bf16[512,256]{0,1:T(8,128)(2,1)} async-done(((bf16[4096,256]{0,1:T(8,128)(2,1)}), bf16[512,256]{0,1:T(8,128)(2,1)}) %reduce-scatter.5.cloned.1.call-update) | async-done | bytes 262160 | tf_op jit(solution)/shard_map/reduce_scatter | solution.py:125
  273.7 1.8 copy.85
  275.5 152.4 %reduce-scatter.7.cloned.1.call-done = bf16[128,768]{1,0:T(8,128)(2,1)} async-done(((bf16[4096,768]{1,0:T(8,128)(2,1)}), bf16[128,768]{1,0:T(8,128)(2,1)}) %reduce-scatter.7.cloned.1.call-update) | async-done | bytes 196624
  427.9 1.1 copy.92
  429.0 0.8 copy.84
  429.8 0.8 copy.83
  430.5 0.8 copy.82
  (56 shorter events, 2.5 us)
Async XLA Ops:
  7.2 1.6 copy-start
  7.2 97.6 %all-gather.2.cloned.1.call-start = ((), (), s32[]{:S(2)}) async-start(), calls=%async_computation.4 | async-start | bytes 4456448 | tf_op jit(solution)/shard_map/all_gather | solution.py:32
  8.8 2.7 copy-start.2
  11.4 2.0 copy-start.6
  11.5 2.1 copy-start.13
  11.5 2.1 copy-start.14
  13.3 108.5 %copy-start.7 = (bf16[256,2,128]{2,0,1:T(8,128)(2,1)}, bf16[256,2,128]{2,0,1:T(8,128)(2,1)S(1)}, u32[]{:S(2)}) copy-start(bf16[256,2,128]{2,0,1:T(8,128)(2,1)S(1)} %copy.61) | copy-start | bytes 393220
  121.5 2.2 copy-start.9
  121.8 3.5 copy-start.11
  125.3 1.2 copy-start.4
  125.3 2.6 copy-start.12
  131.4 0.9 copy-start.5
  156.8 5.2 %copy-start.8 = (bf16[256,2,128]{2,0,1:T(8,128)(2,1)S(1)}, bf16[256,2,128]{2,0,1:T(8,128)(2,1)}, u32[]{:S(2)}) copy-start(bf16[256,2,128]{2,0,1:T(8,128)(2,1)} %copy-done.7) | copy-start | bytes 393220
  156.8 5.2 %copy-start.10 = (bf16[256,2,128]{2,0,1:T(8,128)(2,1)S(1)}, bf16[256,2,128]{2,0,1:T(8,128)(2,1)}, u32[]{:S(2)}) copy-start(bf16[256,2,128]{2,0,1:T(8,128)(2,1)} %copy-done.9) | copy-start | bytes 393220
  158.2 13.5 %all-to-all-start.1 = ((bf16[16,16,512]{2,1,0:T(8,128)(2,1)}), bf16[16,16,512]{2,1,0:T(8,128)(2,1)S(1)}, u32[]{:S(2)}, u32[]{:S(2)}) async-start(bf16[16,16,512]{2,1,0:T(8,128)(2,1)} %copy.79), calls=%async_computation.1 | async-start | bytes 524288 | tf_op jit(solution)/shard_map/all_to_all | solution.py:99
  161.8 111.9 %reduce-scatter.5.cloned.1.call-start = ((), (), s32[]{:S(2)}) async-start(), calls=%async_computation.5 | async-start | bytes 2359296 | tf_op jit(solution)/shard_map/reduce_scatter | solution.py:125
  171.7 1.7 copy-start.1
  173.4 3.1 copy-start.3
  178.6 249.3 %reduce-scatter.7.cloned.1.call-start = ((), (), s32[]{:S(2)}) async-start(), calls=%async_computation.6 | async-start | bytes 6488064
Sparse Core Ops, SparseCore 0:
  13.3 91.4 all-gather.1
  178.7 94.9 reduce-scatter.4
  276.4 151.4 reduce-scatter.6
where the time goes:
time: 439 us; the launch traced here: 438 us
  waiting for transfers between devices  321 us (73%)
  local copies, waits for them, and re-layouts  39.2 us (9%)
  matrix products  30 us (7%)
  blocking collectives  19.8 us (5%)
  between operations  14.2 us (3%)
  other arithmetic  9.41 us (2%)
    unnamed x4, waiting for transfers between devices  152 us
    all_gather x1, waiting for transfers between devices, per_device(): segment = lax.all_gather(key_value, 'doc', axis=0, tiled=True)  84 us
    reduce_scatter x1, waiting for transfers between devices, per_device(): lax.psum_scatter(result.astype(jnp.bfloat16), 'head', scatter_dimension=0...  81.1 us
    all_to_all x1, blocking collectives, per_device(): lax.all_to_all(outbound.astype(jnp.bfloat16), 'doc', split_axis=1, concat...  19.8 us
    unnamed x37, local copies, waits for them, and re-layouts  16.9 us
  transfers between devices with their start and end apart: 4, of which 4 were waited for; matrix products, arithmetic and copies ran while one was open for 7% of the time, Pallas kernels for 0%

commit v1 on v0

--- a/solution.py
+++ b/solution.py
@@ -1,3 +1,4 @@
+import functools
 import math
 import jax
 import jax.numpy as jnp
@@ -5,6 +6,19 @@
 from jax.sharding import PartitionSpec as P
 
 HD = 128
+
+
+def teams_view(u, axis_name):
+    local_out = lax.all_to_all(
+        jnp.stack(jnp.split(u, lax.axis_size(axis_name), axis=1)),
+        axis_name=axis_name,
+        split_axis=0,
+        concat_axis=0,
+    )
+    return jnp.concatenate(local_out, axis=1)
+
+
+node_meet = functools.partial(teams_view, axis_name="doc")
 
 
 def per_device(
@@ -86,9 +100,7 @@
     )
     own_grad = both_grads[:length]
     outbound = both_grads[length:].reshape(2, doc_peers, block_rows, 2 * columns)
-    received = lax.all_to_all(
-        outbound.astype(jnp.bfloat16), "doc", split_axis=1, concat_axis=1, tiled=True
-    ).astype(outbound.dtype)
+    received = node_meet(outbound.astype(jnp.bfloat16)).astype(outbound.dtype)
     chosen_one = (first_partner[:, None] == doc_numbers[None, :]).astype(jnp.float32)
     chosen_two = (second_partner[:, None] == doc_numbers[None, :]).astype(jnp.float32)
     gathered = jnp.einsum("dt,dbf->tbf", chosen_one, received[0], precision=lax.Precision.HIGHEST)

time: 439 us -> 439 us (level)
    unnamed x37 -> x52, local copies, waits for them, and re-layouts: 16.9 us -> 17 us
where the time goes in v1:
time: 439 us; the launch traced here: 438 us
  waiting for transfers between devices  321 us (73%)
  local copies, waits for them, and re-layouts  39.5 us (9%)
  matrix products  29.9 us (7%)
  blocking collectives  19.8 us (5%)
  between operations  14.3 us (3%)
  other arithmetic  9.41 us (2%)
    unnamed x4, waiting for transfers between devices  152 us
    all_gather x1, waiting for transfers between devices, per_device(): segment = lax.all_gather(key_value, 'doc', axis=0, tiled=True)  84 us
    reduce_scatter x1, waiting for transfers between devices, per_device(): lax.psum_scatter(result.astype(jnp.bfloat16), 'head', scatter_dimension=0...  81.1 us
    all_to_all x1, blocking collectives, teams_view(): lax.all_to_all(jnp.stack(jnp.split(u, lax.axis_size(axis_name), axis=1)),...  19.8 us
    unnamed x52, local copies, waits for them, and re-layouts  17 us
  transfers between devices with their start and end apart: 4, of which 4 were waited for; matrix products, arithmetic and copies ran while one was open for 7% of the time, Pallas kernels for 0%

profile of v1, /device:TPU:16, one launch (start us, length us, event | category | flops | bytes accessed | tf_op | source)
XLA Modules:
  0.0 437.7 jit_solution(18151598186662684306)
XLA Ops:
  7.2 1.5 copy-done
  8.8 2.7 fusion.20
  11.5 1.0 fusion.23
  12.5 0.7 pad_maximum_fusion.3
  13.6 0.6 fusion.76
  14.2 0.7 compare_and_fusion
  14.9 0.7 compare_and_fusion.2
  15.5 0.7 compare_and_fusion.1
  16.2 0.7 compare_and_fusion.3
  16.8 0.7 compare_select_fusion
  17.5 0.7 compare_select_fusion.1
  18.3 2.5 fusion.17
  20.8 84.0 %all-gather.2.cloned.1.call-done = bf16[4096,512]{0,1:T(8,128)(2,1)} async-done(((bf16[256,512]{0,1:T(8,128)(2,1)}), bf16[4096,512]{0,1:T(8,128)(2,1)}) %all-gather.2.cloned.1.call-update) | async-done | bytes 4194320 | tf_op jit(solution)/shard_map/all_gather | solution.py:46
  104.8 6.5 %copy.129 = bf16[4096,512]{1,0:T(8,128)(2,1)} copy(bf16[4096,512]{0,1:T(8,128)(2,1)} %all-gather.2.cloned.1.call-done) | data formatting | bytes 8388608 | tf_op jit(solution)/shard_map/all_gather | solution.py:46
  111.3 3.9 gather_fusion.1
  115.3 3.9 gather_fusion
  119.5 0.8 copy.141
  120.5 0.8 copy.140
  121.8 1.9 fusion.78
  123.7 1.6 fusion.29
  125.3 1.2 fusion.80
  126.5 1.4 copy.147
  127.9 1.6 fusion.26
  129.5 1.9 fusion.12
  131.4 0.9 copy-done.5
  132.3 1.2 convolution_multiply_fusion
  133.5 2.3 copy.146
  135.8 1.1 fusion.27
  137.1 19.8 %all_to_all.10 = bf16[16,2,1,16,512]{4,3,2,1,0:T(8,128)(2,1)S(1)} all-to-all(bf16[16,2,1,16,512]{4,3,2,1,0:T(8,128)(2,1)S(1)} %bitcast.182), channel_id=1, replica_groups=mesh['doc'=16,'head'=8,'cuts'=2] {'doc'}, dimensions={0} | all-to-all | bytes 1048576 | tf_op jit(solution)/shard_map/all_to_all | solution.py:12
  157.6 0.9 copy.150
  158.5 3.5 all-to-all-start.1
  162.3 1.6 fusion.16
  163.9 4.3 fusion.79
  168.2 3.8 all-to-all-done.1
  172.0 1.2 fusion.32
  173.1 0.5 copy-done.1
  173.7 3.1 convolution_add_fusion.1
  176.7 2.1 fusion.3
  179.0 4.5 %fusion.1 = bf16[4096,768]{0,1:T(8,128)(2,1)} fusion(bf16[1,1,256,4096]{3,2,1,0:T(8,128)(2,1)S(1)} %copy-done, bf16[256,512]{1,0:T(8,128)(2,1)S(1)} %fusion.32, bf16[256,256]{1,0:T(8,128)(2,1)S(1)} %copy.152), kind=kOutput, calls=%fused_computation.4 | convolution fusion | flops 1614544896 | bytes 8781824 | tf_op jit(solution)/shard_map/dot_general | solution.py:122
  183.5 8.6 %copy.162 = bf16[4096,768]{1,0:T(8,128)(2,1)} copy(bf16[4096,768]{0,1:T(8,128)(2,1)} %fusion.1) | data formatting | bytes 12582912
  192.2 0.7 slice_bitcast_fusion.4
  192.9 81.1 %reduce-scatter.5.cloned.1.call-done = bf16[512,256]{0,1:T(8,128)(2,1)} async-done(((bf16[4096,256]{0,1:T(8,128)(2,1)}), bf16[512,256]{0,1:T(8,128)(2,1)}) %reduce-scatter.5.cloned.1.call-update) | async-done | bytes 262160 | tf_op jit(solution)/shard_map/reduce_scatter | solution.py:137
  274.0 1.8 copy.156
  275.8 152.0 %reduce-scatter.7.cloned.1.call-done = bf16[128,768]{1,0:T(8,128)(2,1)} async-done(((bf16[4096,768]{1,0:T(8,128)(2,1)}), bf16[128,768]{1,0:T(8,128)(2,1)}) %reduce-scatter.7.cloned.1.call-update) | async-done | bytes 196624
  427.8 1.1 copy.163
  428.9 0.8 copy.155
  429.7 0.8 copy.154
  430.5 0.8 copy.153
  (71 shorter events, 2.7 us)
Async XLA Ops:
  7.2 1.6 copy-start
  7.2 97.6 %all-gather.2.cloned.1.call-start = ((), (), s32[]{:S(2)}) async-start(), calls=%async_computation.4 | async-start | bytes 4456448 | tf_op jit(solution)/shard_map/all_gather | solution.py:46
  8.8 2.7 copy-start.2
  11.4 2.0 copy-start.6
  11.5 2.1 copy-start.13
  11.5 2.1 copy-start.14
  13.3 108.4 %copy-start.7 = (bf16[256,2,128]{2,0,1:T(8,128)(2,1)}, bf16[256,2,128]{2,0,1:T(8,128)(2,1)S(1)}, u32[]{:S(2)}) copy-start(bf16[256,2,128]{2,0,1:T(8,128)(2,1)S(1)} %copy.133) | copy-start | bytes 393220
  121.5 2.2 copy-start.9
  121.8 3.5 copy-start.11
  125.3 1.2 copy-start.4
  125.3 2.6 copy-start.12
  131.4 0.9 copy-start.5
  156.9 5.4 %copy-start.8 = (bf16[256,2,128]{2,0,1:T(8,128)(2,1)S(1)}, bf16[256,2,128]{2,0,1:T(8,128)(2,1)}, u32[]{:S(2)}) copy-start(bf16[256,2,128]{2,0,1:T(8,128)(2,1)} %copy-done.7) | copy-start | bytes 393220
  156.9 5.4 %copy-start.10 = (bf16[256,2,128]{2,0,1:T(8,128)(2,1)S(1)}, bf16[256,2,128]{2,0,1:T(8,128)(2,1)}, u32[]{:S(2)}) copy-start(bf16[256,2,128]{2,0,1:T(8,128)(2,1)} %copy-done.9) | copy-start | bytes 393220
  158.5 13.5 %all-to-all-start.1 = ((bf16[16,16,512]{2,1,0:T(8,128)(2,1)}), bf16[16,16,512]{2,1,0:T(8,128)(2,1)S(1)}, u32[]{:S(2)}, u32[]{:S(2)}) async-start(bf16[16,16,512]{2,1,0:T(8,128)(2,1)} %copy.150), calls=%async_computation.1 | async-start | bytes 524288 | tf_op jit(solution)/shard_map/all_to_all | solution.py:111
  162.0 112.0 %reduce-scatter.5.cloned.1.call-start = ((), (), s32[]{:S(2)}) async-start(), calls=%async_computation.5 | async-start | bytes 2359296 | tf_op jit(solution)/shard_map/reduce_scatter | solution.py:137
  172.0 1.7 copy-start.1
  173.6 3.1 copy-start.3
  178.9 249.0 %reduce-scatter.7.cloned.1.call-start = ((), (), s32[]{:S(2)}) async-start(), calls=%async_computation.6 | async-start | bytes 6488064
Sparse Core Ops, SparseCore 0:
  13.3 91.4 all-gather.1
  179.0 94.9 reduce-scatter.4
  276.7 151.0 reduce-scatter.6
